TPU v7x, 32 devices: a whole 2x2x4 slice. The times are simulated.
32 devices in a mesh: cases: 2 (over x), bus: 16 (over z, y, core).
Axes of the slice: x: 2, y: 2, z: 4, core: 2. Of those that a mesh axis runs over, the one named last changes fastest.
Arguments:
- ptdf: bfloat16 [20480, 10240], P('bus'), may hold values from -0.078125 to 0.078125
- line_limit: float32 [20480], P('bus'), may hold values from 1 to 8
- gen_cost: float32 [12288], P('bus'), may hold values from 0.1 to 2
- gen_max: float32 [12288], P('bus'), may hold values from 0.5 to 4
- gen_owner: int32 [12288, 1], P('bus'), may hold values from 0 to 15; in each aligned block of 768 rows (0 to 767, 768 to 1535, ...) at most 144 rows name the same one
- gen_local: int32 [12288], P('bus'), may hold values from 0 to 639
- availability: float32 [24576, 128], P(('cases', 'bus')), parts along dimension 0, may hold values from 0 to 1
- demand: float32 [20480, 128], P(('cases', 'bus')), parts along dimension 0, may hold values from 0.5 to 2.5
- dispatch: float32 [24576, 128], P(('cases', 'bus')), parts along dimension 0, may hold values from 0 to 2
- balance_price: float32 [256], P('cases'), parts along dimension 0, may hold values from -6 to 6
- line_price: float32 [40960, 128], P(('cases', 'bus')), parts along dimension 0, may hold values from -4 to 4
Outputs:
- dispatch_out: float32 [24576, 128], P(('cases', 'bus')), parts along dimension 0
- balance_out: float32 [256], P('cases'), parts along dimension 0
- line_out: float32 [40960, 128], P(('cases', 'bus')), parts along dimension 0
There are 2 independent parts, one for each index of `cases`. A program takes and returns all parts, laid end to end along the dimension named above; an argument that names none is the same for every part. Nothing has to cross between parts.
Inputs may be any that keep to these rules, and one draw needn't show every extreme that they name: `gen_owner`: among the 768 generators of one device (aligned blocks of rows), no owner is named more than 144 times, a bound that some block reaches.
All inputs are finite; a program needn't handle non-finite values.
Results may differ from a plain program's by a relative error of at most 0.0036.
Values may be sent and summed in bfloat16 or wider, within the bound.
A program may use at most 128 MiB of HBM per device.

v0:
```python
import jax
import jax.numpy as jnp
from jax import lax
from jax.sharding import PartitionSpec as P

ITERS = 2


tau_step = 0.2
sigma_step = 0.15


def local(
    ptdf,
    line_limit,
    gen_cost,
    gen_max,
    gen_owner,
    gen_local,
    availability,
    demand,
    dispatch,
    balance_price,
    line_price,
):
    devices = lax.axis_size("bus")
    position = lax.axis_index("bus")
    bus_rows = demand.shape[0]
    all_buses = bus_rows * devices
    gen_rows = dispatch.shape[0]
    hour_count = dispatch.shape[1]
    capacity = max(2, 3 * gen_rows // devices)
    owner = gen_owner[:, 0]
    global_bus = owner * bus_rows + gen_local
    every_bus = lax.all_gather(global_bus, "bus", axis=0, tiled=True)
    owner_hits = (owner[:, None] == jnp.arange(devices, dtype=jnp.int32)[None, :]).astype(jnp.int32)
    owner_rank = jnp.sum((jnp.cumsum(owner_hits, axis=0) - owner_hits) * owner_hits, axis=1)
    slot_index = owner * capacity + owner_rank
    source_bus = every_bus.reshape(devices, gen_rows)
    mine = (source_bus // bus_rows == position).astype(jnp.int32)
    mine_rank = jnp.cumsum(mine, axis=1) - mine
    rank_ids = jnp.arange(capacity, dtype=jnp.int32)
    rank_match = mine[:, :, None] * (mine_rank[:, :, None] == rank_ids[None, None, :]).astype(
        jnp.int32
    )
    local_bus = source_bus - position * bus_rows
    arrived_buses = (
        jnp.sum(rank_match * local_bus[:, :, None], axis=1)
        + (1 - jnp.sum(rank_match, axis=1)) * bus_rows
    )
    flat_buses = arrived_buses.reshape(-1)
    pick_rows = jnp.minimum(flat_buses, bus_rows - 1)
    upper = gen_max[:, None] * availability
    limit = line_limit[:, None]
    for iteration in range(ITERS):
        line_half = line_price.astype(jnp.bfloat16)
        shadow = lax.psum_scatter(
            lax.dot_general(
                ptdf, line_half, (((0,), (0,)), ((), ())), preferred_element_type=jnp.float32
            ),
            "bus",
            scatter_dimension=0,
            tiled=True,
        )
        outgoing = jnp.take(shadow, pick_rows, axis=0).reshape(devices, capacity, hour_count)
        returned = lax.all_to_all(outgoing, "bus", split_axis=0, concat_axis=0, tiled=True)
        bus_price = jnp.take(returned.reshape(devices * capacity, hour_count), slot_index, axis=0)
        price = bus_price + balance_price[None, :]
        updated = jnp.clip(dispatch - tau_step * (gen_cost[:, None] + price), 0.0, upper)
        extra = 2.0 * updated - dispatch
        full_sums = jax.ops.segment_sum(extra, global_bus, num_segments=all_buses)
        injection = lax.psum_scatter(full_sums, "bus", scatter_dimension=0, tiled=True) - demand
        balance = lax.psum(jnp.sum(injection, axis=0), "bus")
        balance_price = balance_price + sigma_step * balance / all_buses
        flow = jnp.dot(
            ptdf,
            lax.all_gather(injection.astype(jnp.bfloat16), "bus", axis=0, tiled=True),
            preferred_element_type=jnp.float32,
        )
        shifted = line_price + sigma_step * flow
        line_price = shifted - sigma_step * jnp.clip(shifted / sigma_step, -limit, limit)
        dispatch = updated
    return (dispatch, balance_price, line_price)


def solution(mesh):
    return jax.shard_map(
        local,
        mesh=mesh,
        in_specs=(
            P("bus", None),
            P("bus"),
            P("bus"),
            P("bus"),
            P("bus", None),
            P("bus"),
            P(("cases", "bus"), None),
            P(("cases", "bus"), None),
            P(("cases", "bus"), None),
            P("cases"),
            P(("cases", "bus"), None),
        ),
        out_specs=(P(("cases", "bus"), None), P("cases"), P(("cases", "bus"), None)),
        check_vma=False,
    )
```

profile of v0, /device:TPU:17, one launch (start us, length us, event | category | flops | bytes accessed | tf_op | source)
XLA Modules:
  0.0 590.9 jit_solution(11332282485617281092)
XLA Ops:
  7.2 0.0 reduce-scatter.5.cloned.1.call-start
  7.2 13.8 %fusion.24 = f32[10240,128]{1,0:T(8,128)} fusion(bf16[1280,10240]{1,0:T(8,128)(2,1)} %param.15, f32[1280,128]{1,0:T(8,128)} %param.25), kind=kOutput, calls=%fused_computation.42 | convolution fusion | flops 3355607040 | bytes 32112640 | tf_op jit(solution)/shard_map/dot_general | solution.py:58
  21.1 0.7 copy-done.11
  21.8 16.6 %all-gather = s32[16,1,768]{2,1,0:T(1,128)S(1)} all-gather(s32[1,1,768]{2,1,0:T(1,128)S(1)} %reshape.201), channel_id=1, replica_groups=mesh['cases'=2,'bus'=16] {'bus'}, dimensions={0}, use_global_device_ids=true | all-gather | bytes 52224 | tf_op jit(solution)/shard_map/all_gather | solution.py:35
  38.4 0.1 and.28
  38.6 1.7 reduce-window.14
  40.3 0.3 slice_reduce_fusion
  40.6 0.1 bitcast_subtract_fusion
  40.7 1.6 select_reduce_fusion
  42.3 0.1 min.36
  42.4 56.2 %reduce-scatter.5.cloned.1.call-done = f32[640,128]{1,0:T(8,128)} async-done(((f32[10240,128]{1,0:T(8,128)}), f32[640,128]{1,0:T(8,128)}) %reduce-scatter.5.cloned.1.call-update) | async-done | bytes 327696 | tf_op jit(solution)/shard_map/reduce_scatter | solution.py:57
  98.7 4.9 gather_fusion
  103.6 2.0 broadcast_select_fusion.1
  105.6 6.4 %all-to-all-start = ((f32[16,144,128]{2,1,0:T(8,128)}), f32[16,144,128]{2,1,0:T(8,128)S(1)}, u32[]{:S(2)}, u32[]{:S(2)}) async-start(f32[16,144,128]{2,1,0:T(8,128)} %bitcast.3), calls=%async_computation.1 | async-start | bytes 2359296 | tf_op jit(solution)/shard_map/all_to_all | solution.py:66
  112.1 0.0 reduce-scatter.7.cloned.1.call-start
  112.1 1.7 reduce-window.16
  113.9 0.3 slice_reduce_fusion.1
  114.1 0.1 fusion.32
  114.3 25.3 %all-to-all-done = f32[16,144,128]{2,1,0:T(8,128)S(1)} async-done(((f32[16,144,128]{2,1,0:T(8,128)}), f32[16,144,128]{2,1,0:T(8,128)S(1)}, u32[]{:S(2)}, u32[]{:S(2)}) %all-to-all-start) | async-done | bytes 1179680 | tf_op jit(solution)/shard_map/all_to_all | solution.py:66
  139.6 1.6 gather_fusion.1
  141.2 0.4 fusion.18
  141.6 8.7 %scatter_custom_fusion = f32[10240,128]{1,0:T(8,128)} fusion(s32[768]{0:T(1024)S(1)} %multiply_add_fusion, f32[]{:T(128)} %constant.29.clone.1, f32[768,128]{1,0:T(8,128)S(1)} %copy-done.1, f32[768,128]{1,0:T(8,128)S(1)} %fusion.18, f32[]{:T(128)} %constant.66.clone.1), kind=kCustom, calls=%fused_computation.13 | custom fusion | flops 294912 | bytes 6029320 | tf_op jit(solution)/shard_map/scatter-add | solution.py:71
  150.3 0.0 all-gather.4.cloned.1.call-start
  150.4 76.2 %reduce-scatter.7.cloned.1.call-done = f32[640,128]{1,0:T(8,128)} async-done(((f32[10240,128]{1,0:T(8,128)}), f32[640,128]{1,0:T(8,128)}) %reduce-scatter.7.cloned.1.call-update) | async-done | bytes 327696 | tf_op jit(solution)/shard_map/reduce_scatter | solution.py:72
  226.6 1.7 subtract_reduce_fusion.1
  228.3 0.2 reduce-scatter.9.cloned.1.call-start
  228.5 0.2 copy.52
  228.8 44.3 %all-gather.4.cloned.1.call-done = bf16[10240,128]{1,0:T(8,128)(2,1)} async-done(((bf16[640,128]{1,0:T(8,128)(2,1)}), bf16[10240,128]{1,0:T(8,128)(2,1)}) %all-gather.4.cloned.1.call-update) | async-done | bytes 2621456 | tf_op jit(solution)/shard_map/all_gather | solution.py:77
  273.1 13.8 %multiply_subtract_fusion.1 = f32[1280,128]{0,1:T(8,128)S(1)} fusion(f32[1280,128]{0,1:T(8,128)S(1)} %copy.52, bf16[10240,128]{1,0:T(8,128)(2,1)} %all-gather.4.cloned.1.call-done, bf16[1280,10240]{1,0:T(8,128)(2,1)} %param.15, f32[1280]{0:T(1024)S(1)} %neg.5, f32[1280]{0:T(1024)S(1)} %copy-done.7), kind=kOutput, calls=%fused_computation.22 | convolution fusion | flops 3356590080 | bytes 30156800 | tf_op jit(solution)/shard_map/dot_general | solution.py:75
  286.9 14.3 %convolution_bitcast_fusion = f32[10240,128]{0,1:T(8,128)} fusion(bf16[1280,10240]{1,0:T(8,128)(2,1)} %param.15, f32[1280,128]{0,1:T(8,128)S(1)} %multiply_subtract_fusion.1), kind=kOutput, calls=%fused_computation.6 | convolution fusion | flops 3355607040 | bytes 32112640 | tf_op jit(solution)/shard_map/dot_general | solution.py:58
  301.3 75.7 %reduce-scatter.9.cloned.1.call-done = f32[640,128]{0,1:T(8,128)} async-done(((f32[10240,128]{0,1:T(8,128)}), f32[640,128]{0,1:T(8,128)}) %reduce-scatter.9.cloned.1.call-update) | async-done | bytes 327696 | tf_op jit(solution)/shard_map/reduce_scatter | solution.py:57
  376.9 1.1 copy.53
  378.1 3.9 gather_fusion.2
  382.0 2.0 broadcast_select_fusion
  384.0 6.7 %all-to-all-start.1 = ((f32[16,144,128]{2,1,0:T(8,128)}), f32[16,144,128]{2,1,0:T(8,128)S(1)}, u32[]{:S(2)}, u32[]{:S(2)}) async-start(f32[16,144,128]{2,1,0:T(8,128)} %bitcast.7), calls=%async_computation.4 | async-start | bytes 2359296 | tf_op jit(solution)/shard_map/all_to_all | solution.py:66
  390.7 0.0 reduce-scatter.11.cloned.1.call-start
  390.8 44.4 %psum.14 = f32[128]{0:T(128)S(1)} all-reduce(f32[128]{0:T(128)S(1)} %get-tuple-element.28), channel_id=1, replica_groups=mesh['cases'=2,'bus'=16] {'bus'}, use_global_device_ids=true, to_apply=%region_12.15 | all-reduce | flops 128 | bytes 1024 | tf_op jit(solution)/shard_map/psum | solution.py:73
  435.1 1.6 gather_fusion.3
  436.7 0.4 fusion.13
  437.1 8.7 %scatter_custom_fusion.1 = f32[10240,128]{1,0:T(8,128)} fusion(s32[768]{0:T(1024)S(1)} %multiply_add_fusion, f32[]{:T(128)} %constant.29.clone.1, f32[768,128]{1,0:T(8,128)S(1)} %fusion.18, f32[768,128]{1,0:T(8,128)S(1)} %fusion.13, f32[]{:T(128)} %constant.66.clone.1), kind=kCustom, calls=%fused_computation.11 | custom fusion | flops 294912 | bytes 6029320 | tf_op jit(solution)/shard_map/scatter-add | solution.py:71
  445.9 0.0 all-gather.6.cloned.1.call-start
  445.9 76.8 %reduce-scatter.11.cloned.1.call-done = f32[640,128]{1,0:T(8,128)} async-done(((f32[10240,128]{1,0:T(8,128)}), f32[640,128]{1,0:T(8,128)}) %reduce-scatter.11.cloned.1.call-update) | async-done | bytes 327696 | tf_op jit(solution)/shard_map/reduce_scatter | solution.py:72
  522.8 1.7 subtract_convert_fusion
  524.5 23.8 %psum.15 = f32[128]{0:T(128)S(1)} all-reduce(f32[128]{0:T(128)S(1)} %get-tuple-element.27), channel_id=1, replica_groups=mesh['cases'=2,'bus'=16] {'bus'}, use_global_device_ids=true, to_apply=%region_16.19 | all-reduce | flops 128 | bytes 1024 | tf_op jit(solution)/shard_map/psum | solution.py:73
  548.3 0.5 multiply_add_fusion.1
  548.8 20.4 %all-gather.6.cloned.1.call-done = bf16[10240,128]{1,0:T(8,128)(2,1)} async-done(((bf16[640,128]{1,0:T(8,128)(2,1)}), bf16[10240,128]{1,0:T(8,128)(2,1)}) %all-gather.6.cloned.1.call-update) | async-done | bytes 2621456 | tf_op jit(solution)/shard_map/all_gather | solution.py:77
  569.2 13.8 %multiply_subtract_fusion = f32[1280,128]{0,1:T(8,128)S(1)} fusion(f32[1280,128]{0,1:T(8,128)S(1)} %multiply_subtract_fusion.1, bf16[10240,128]{1,0:T(8,128)(2,1)} %all-gather.6.cloned.1.call-done, bf16[1280,10240]{1,0:T(8,128)(2,1)} %param.15, f32[1280]{0:T(1024)S(1)} %neg.5, f32[1280]{0:T(1024)S(1)} %copy-done.7), kind=kOutput, calls=%fused_computation.21 | convolution fusion | flops 3356590080 | bytes 30156800 | tf_op jit(solution)/shard_map/dot_general | solution.py:75
  583.0 1.1 copy.54
  (52 shorter events, 0.4 us)
Async XLA Ops:
  7.2 91.5 %reduce-scatter.5.cloned.1.call-start = ((), (), s32[]{:S(2)}) async-start(), calls=%async_computation.6 | async-start | bytes 5570560 | tf_op jit(solution)/shard_map/reduce_scatter | solution.py:57
  21.0 0.7 copy-start.11
  21.0 0.7 copy-start.10
  103.5 37.6 %copy-start.1 = (f32[768,128]{1,0:T(8,128)S(1)}, f32[768,128]{1,0:T(8,128)}, u32[]{:S(2)}) copy-start(f32[768,128]{1,0:T(8,128)} %param.23) | copy-start | bytes 1179652
  103.5 37.6 %copy-start.3 = (f32[768,128]{1,0:T(8,128)S(1)}, f32[768,128]{1,0:T(8,128)}, u32[]{:S(2)}) copy-start(f32[768,128]{1,0:T(8,128)} %param.21) | copy-start | bytes 1179652
  103.6 37.6 %copy-start.8 = (f32[768]{0:T(1024)S(1)}, f32[768]{0:T(1024)}, u32[]{:S(2)}) copy-start(f32[768]{0:T(1024)} %param.17) | copy-start | bytes 9220
  103.6 37.6 %copy-start.9 = (f32[768]{0:T(1024)S(1)}, f32[768]{0:T(1024)}, u32[]{:S(2)}) copy-start(f32[768]{0:T(1024)} %param.18) | copy-start | bytes 9220
  103.6 37.6 %copy-start.12 = (f32[128]{0:T(128)S(1)}, f32[128]{0:T(128)}, u32[]{:S(2)}) copy-start(f32[128]{0:T(128)} %param.24) | copy-start | bytes 1540
  105.6 33.9 %all-to-all-start = ((f32[16,144,128]{2,1,0:T(8,128)}), f32[16,144,128]{2,1,0:T(8,128)S(1)}, u32[]{:S(2)}, u32[]{:S(2)}) async-start(f32[16,144,128]{2,1,0:T(8,128)} %bitcast.3), calls=%async_computation.1 | async-start | bytes 2359296 | tf_op jit(solution)/shard_map/all_to_all | solution.py:66
  112.1 114.5 %reduce-scatter.7.cloned.1.call-start = ((), (), s32[]{:S(2)}) async-start(), calls=%async_computation.7 | async-start | bytes 5570560 | tf_op jit(solution)/shard_map/reduce_scatter | solution.py:72
  141.6 85.0 %copy-start.5 = (f32[640,128]{1,0:T(8,128)S(1)}, f32[640,128]{1,0:T(8,128)}, u32[]{:S(2)}) copy-start(f32[640,128]{1,0:T(8,128)} %param.22) | copy-start | bytes 983044
  141.6 87.0 %copy-start = (f32[1280,128]{1,0:T(8,128)S(1)}, f32[1280,128]{1,0:T(8,128)}, u32[]{:S(2)}) copy-start(f32[1280,128]{1,0:T(8,128)} %param.25) | copy-start | bytes 1966084
  150.3 78.5 %copy-start.7 = (f32[1280]{0:T(1024)S(1)}, f32[1280]{0:T(1024)}, u32[]{:S(2)}) copy-start(f32[1280]{0:T(1024)} %param.16) | copy-start | bytes 15364
  150.3 122.8 %all-gather.4.cloned.1.call-start = ((), (), s32[]{:S(2)}) async-start(), calls=%async_computation.8 | async-start | bytes 2785280 | tf_op jit(solution)/shard_map/all_gather | solution.py:77
  228.3 148.6 %reduce-scatter.9.cloned.1.call-start = ((), (), s32[]{:S(2)}) async-start(), calls=%async_computation.9 | async-start | bytes 5570560 | tf_op jit(solution)/shard_map/reduce_scatter | solution.py:57
  384.0 52.7 %copy-start.4 = (f32[768,128]{1,0:T(8,128)S(1)}, f32[768,128]{1,0:T(8,128)}, u32[]{:S(2)}) copy-start(f32[768,128]{1,0:T(8,128)} %param.21) | copy-start | bytes 1179652
  384.0 51.1 %all-to-all-start.1 = ((f32[16,144,128]{2,1,0:T(8,128)}), f32[16,144,128]{2,1,0:T(8,128)S(1)}, u32[]{:S(2)}, u32[]{:S(2)}) async-start(f32[16,144,128]{2,1,0:T(8,128)} %bitcast.7), calls=%async_computation.4 | async-start | bytes 2359296 | tf_op jit(solution)/shard_map/all_to_all | solution.py:66
  390.7 132.0 %reduce-scatter.11.cloned.1.call-start = ((), (), s32[]{:S(2)}) async-start(), calls=%async_computation.10 | async-start | bytes 5570560 | tf_op jit(solution)/shard_map/reduce_scatter | solution.py:72
  437.1 8.8 %copy-start.2 = (f32[768,128]{1,0:T(8,128)}, f32[768,128]{1,0:T(8,128)S(1)}, u32[]{:S(2)}) copy-start(f32[768,128]{1,0:T(8,128)S(1)} %fusion.13) | copy-start | bytes 1179652
  437.1 85.7 %copy-start.6 = (f32[640,128]{1,0:T(8,128)S(1)}, f32[640,128]{1,0:T(8,128)}, u32[]{:S(2)}) copy-start(f32[640,128]{1,0:T(8,128)} %param.22) | copy-start | bytes 983044
  445.9 123.3 %all-gather.6.cloned.1.call-start = ((), (), s32[]{:S(2)}) async-start(), calls=%async_computation.11 | async-start | bytes 2785280 | tf_op jit(solution)/shard_map/all_gather | solution.py:77
Sparse Core Ops, SparseCore 0:
  21.2 77.4 reduce-scatter.4
  150.4 76.0 reduce-scatter.6
  229.5 43.6 all-gather.3
  301.4 75.4 reduce-scatter.8
  446.0 76.7 reduce-scatter.10
  525.5 43.7 all-gather.5
where the time goes:
time: 594 us; the launch traced here: 591 us
  waiting for transfers between devices  375 us (63%)
  blocking collectives  84.8 us (14%)
  matrix products  55.7 us (9%)
  other arithmetic  31.6 us (5%)
  local copies, waits for them, and re-layouts  15.7 us (3%)
  between operations  14.5 us (2%)
  starting transfers between devices  13.5 us (2%)
    reduce_scatter x2, waiting for transfers between devices, local(): lax.psum_scatter(full_sums, 'bus', scatter_dimension=0, tiled=True) - demand  153 us
    reduce_scatter x2, waiting for transfers between devices, local(): lax.psum_scatter(lax.dot_general(ptdf, line_half, (((0,), (0,)), ((), ())...  132 us
    psum x2, blocking collectives, local(): balance = lax.psum(jnp.sum(injection, axis=0), 'bus')  68.2 us
    all_gather x2, waiting for transfers between devices, local(): lax.all_gather(injection.astype(jnp.bfloat16), 'bus', axis=0, tiled=True)  64.8 us
    dot_general x2, matrix products, local(): lax.dot_general(ptdf, line_half, (((0,), (0,)), ((), ())), preferred_elem...  28.2 us
    dot_general x2, matrix products, local(): jnp.dot(ptdf, lax.all_gather(injection.astype(jnp.bfloat16), 'bus', axis=...  27.6 us
    all_to_all x2, waiting for transfers between devices, local(): lax.all_to_all(outgoing, 'bus', split_axis=0, concat_axis=0, tiled=True)  25.3 us
    scatter-add x2, other arithmetic, local(): full_sums = jax.ops.segment_sum(extra, global_bus, num_segments=all_buses)  17.5 us
  transfers between devices with their start and end apart: 8, of which 7 were waited for; matrix products, arithmetic and copies ran while one was open for 1% of the time, Pallas kernels for 0%

commit v1 on v0

v1 whole, which is shorter than its diff:
```python
import functools

import jax
import jax.numpy as jnp
from jax import lax
from jax.experimental import pallas as pl
from jax.experimental.pallas import tpu as pltpu
from jax.sharding import PartitionSpec as P

ITERS = 2


tau_step = 0.2
sigma_step = 0.15

BF = jnp.bfloat16
F32 = jnp.float32
NT = (((1,), (1,)), ((), ()))
TN = (((0,), (0,)), ((), ()))


def dot(a, b, dims=(((1,), (0,)), ((), ()))):
    return lax.dot_general(a, b, dims, preferred_element_type=F32)


def split(x):
    high = x.astype(BF)
    return high, (x - high.astype(F32)).astype(BF)


def loop(low, high, body):
    lax.fori_loop(low, high, lambda i, c: (body(i), c)[1], 0)


def kernel(
    n,
    capacity,
    flat,
    ptdf,
    limit,
    gen_rows_in,
    gen_max,
    availability,
    demand,
    dispatch,
    balance_in,
    line_in,
    dispatch_out,
    balance_out,
    line_out,
    pt,
    line_t,
    part_tx,
    part,
    core_rx,
    y_tx,
    y_rx,
    z_tx,
    z_rx,
    shadow_t,
    inj_all,
    inj_acc,
    flow,
    bal,
    pick,
    gen_tx,
    gen_rx,
    seat,
    cost,
    upper,
    state,
    ret_tx,
    ret_rx,
    load_sem,
    s1,
    r1,
    s2,
    r2,
    s3,
    r3,
    s4,
    r4,
    s5,
    r5,
    s6,
    r6,
    sa,
    ra,
    sb,
    rb,
):
    lines = pt.shape[1]
    buses = pt.shape[2]
    hours = line_in.shape[1]
    gens = dispatch.shape[0]
    wide = gen_tx.shape[2]
    depth = n // 4
    me = lax.axis_index("bus")
    c = lax.rem(me, 2)
    y = lax.rem(lax.div(me, 2), 2)
    z = lax.div(me, 4)

    def at(zz, yy, cc):
        return zz * 4 + yy * 2 + cc

    def z_to(k):
        return lax.rem(z + 1 + k, depth)

    def z_from(k):
        return lax.rem(z + 2 * depth - 1 - k, depth)

    core_peer = at(z, y, 1 - c)
    y_peer = at(z, 1 - y, c)

    def load(o):
        if flat:
            src = ptdf.at[:, pl.ds(pl.multiple_of(o * buses, 128), buses)]
        else:
            src = ptdf.at[o]
        return pltpu.make_async_copy(src, pt.at[o], load_sem.at[o])

    def remote(src, dst, send, recv, target):
        return pltpu.make_async_remote_copy(
            src_ref=src,
            dst_ref=dst,
            send_sem=send,
            recv_sem=recv,
            device_id={"bus": target},
            device_id_type=pl.DeviceIdType.MESH,
        )

    def owners(k):
        zt = z_to(k)
        return (at(zt, 1 - y, 1 - c), at(zt, 1 - y, c), at(zt, y, 1 - c), at(zt, y, c))

    def start_loads(k):
        a, b, _, _ = owners(k)
        load(a).start()
        load(b).start()

    def start_loads_near(k):
        _, _, a, b = owners(k)
        load(a).start()
        load(b).start()

    loop(0, depth, start_loads)
    loop(0, depth, start_loads_near)

    barrier = pltpu.get_barrier_semaphore()

    def greet(d):
        pl.semaphore_signal(
            barrier,
            inc=1,
            device_id={"bus": lax.rem(me + d, n)},
            device_id_type=pl.DeviceIdType.MESH,
        )

    loop(1, n, greet)
    pl.semaphore_wait(barrier, n - 1)

    line_out[...] = line_in[...]
    balance_out[...] = balance_in[...]

    owner_row = gen_rows_in[0:1, :]
    local_row = gen_rows_in[1:2, :]
    cost_row = gen_rows_in[2:3, :]
    owner_ids = lax.broadcasted_iota(jnp.int32, (n, gens), 0).astype(F32)
    hits = (owner_ids == owner_row).astype(F32)
    before = (
        lax.broadcasted_iota(jnp.int32, (gens, gens), 0)
        < lax.broadcasted_iota(jnp.int32, (gens, gens), 1)
    ).astype(F32)
    counts = dot(hits.astype(BF), before.astype(BF))
    rank_row = jnp.sum(counts * hits, axis=0, keepdims=True)
    local_high = jnp.floor(local_row * (1.0 / 16.0))
    local_low = local_row - 16.0 * local_high
    cost_a = cost_row.astype(BF).astype(F32)
    cost_b = (cost_row - cost_a).astype(BF).astype(F32)
    cost_c = cost_row - cost_a - cost_b
    facts = jnp.concatenate(
        [
            local_high,
            local_low,
            jnp.ones_like(local_row),
            cost_a,
            cost_b,
            cost_c,
            jnp.zeros((10, gens), F32),
        ],
        axis=0,
    ).astype(BF)
    goods = jnp.concatenate(
        [dispatch[...].astype(BF), (gen_max[...] * availability[...]).astype(BF)], axis=1
    )
    slot_ids = lax.broadcasted_iota(jnp.int32, (wide, gens), 0).astype(F32)

    def gen_copy(d):
        return remote(
            gen_tx.at[d], gen_rx.at[d], sa.at[d], ra.at[d], lax.rem(me + d, n)
        )

    def send_gens(d):
        o = lax.rem(me + d, n).astype(F32)
        where = jnp.where(owner_row == o, rank_row, -1.0)
        chosen = (slot_ids == where).astype(F32).astype(BF)
        pick[d] = chosen[:capacity]
        body = dot(chosen[:capacity], goods).astype(BF)
        tail = dot(facts, chosen, NT).astype(BF)

        @pl.when(d > 0)
        def _():
            gen_tx[d, :capacity] = body
            gen_tx[d, capacity:] = tail
            gen_copy(d).start()

        @pl.when(d == 0)
        def _():
            gen_rx[0, :capacity] = body
            gen_rx[0, capacity:] = tail

    loop(0, n, send_gens)

    def take_gens(d):
        @pl.when(d > 0)
        def _():
            gen_copy(d).wait_recv()

        eye = (
            lax.broadcasted_iota(jnp.int32, (capacity, wide), 0)
            == lax.broadcasted_iota(jnp.int32, (capacity, wide), 1)
        ).astype(F32).astype(BF)
        columns = dot(eye, gen_rx[d, capacity:], NT)
        bus = jnp.where(
            columns[:, 2:3] > 0.5, columns[:, 0:1] * 16.0 + columns[:, 1:2], -1.0
        )
        ids = lax.broadcasted_iota(jnp.int32, (capacity, buses), 1).astype(F32)
        seat[d] = (ids == bus).astype(F32).astype(BF)
        cost[d] = jnp.broadcast_to(
            columns[:, 3:4] + columns[:, 4:5] + columns[:, 5:6], (capacity, hours)
        )
        state[d] = gen_rx[d, :capacity, :hours].astype(F32)
        upper[d] = gen_rx[d, :capacity, hours:].astype(F32)

    def c1(j):
        return remote(part_tx.at[j], core_rx.at[j], s1.at[j], r1.at[j], core_peer)

    def c2(k):
        return remote(y_tx.at[k], y_rx.at[k], s2.at[k], r2.at[k], y_peer)

    def c3(k):
        return remote(z_tx.at[k], z_rx.at[k], s3.at[k], r3.at[k], at(z_to(k), y, c))

    def c4(k):
        own = inj_all.at[me]
        return remote(own, own, s4.at[k], r4.at[k], at(z_to(k), y, c))

    def c5(k):
        block = inj_all.at[at(z_from(k), y, c)]
        return remote(block, block, s5.at[k], r5.at[k], y_peer)

    def c6(k):
        block = inj_all.at[at(z_from(k), y, c)]
        return remote(block, block, s6.at[k], r6.at[k], core_peer)

    def c6y(k):
        block = inj_all.at[at(z_from(k), 1 - y, c)]
        return remote(block, block, s6.at[depth + k], r6.at[depth + k], core_peer)

    def ret_copy(d):
        return remote(
            ret_tx.at[d], ret_rx.at[d], sb.at[d], rb.at[d], lax.rem(me + n - d, n)
        )

    def iterate(it):
        line_t[...] = jnp.transpose(line_out[...]).astype(BF)

        def partial(o):
            @pl.when(it == 0)
            def _():
                load(o).wait()

            return dot(line_t[...], pt[o])

        def step(j, send_to, keep):
            part_tx[j] = partial(send_to).astype(BF)
            c1(j).start()
            part[j] = partial(keep)

        def far_finish(k):
            c1(k).wait_recv()
            y_tx[k] = (part[k] + core_rx[k].astype(F32)).astype(BF)
            c2(k).start()

        def far(k):
            a, b, _, _ = owners(k)
            step(k, a, b)

            @pl.when(k > 0)
            def _():
                far_finish(k - 1)

        def near(k):
            _, _, a, b = owners(k)
            step(depth + k, a, b)

            @pl.when(k == 0)
            def _():
                far_finish(depth - 1)

        def near_finish(k):
            c1(depth + k).wait_recv()
            c2(k).wait_recv()
            total = (
                part[depth + k]
                + core_rx[depth + k].astype(F32)
                + y_rx[k].astype(F32)
            )

            @pl.when(k < depth - 1)
            def _():
                z_tx[k] = total.astype(BF)
                c3(k).start()

            @pl.when(k == depth - 1)
            def _():
                shadow_t[...] = total

        loop(0, depth, far)
        loop(0, depth, near)
        loop(0, depth, near_finish)

        @pl.when(it == 0)
        def _():
            loop(0, n, take_gens)

        def add_z(k):
            c3(k).wait_recv()
            shadow_t[...] += z_rx[k].astype(F32)

        loop(0, depth - 1, add_z)

        def sent_rs(k):
            c1(k).wait_send()
            c1(depth + k).wait_send()
            c2(k).wait_send()

        loop(0, depth, sent_rs)
        loop(0, depth - 1, lambda k: c3(k).wait_send())

        high, low = split(shadow_t[...])
        both = jnp.concatenate([high, low], axis=0)
        inj_acc[...] = jnp.zeros_like(inj_acc)

        def update(d):
            found = dot(seat[d], both, NT)
            price = found[:, :hours] + found[:, hours:] + balance_out[...]
            now = state[d]
            updated = jnp.clip(now - tau_step * (cost[d] + price), 0.0, upper[d])
            high, low = split(2.0 * updated - now)
            inj_acc[...] += dot(seat[d], jnp.concatenate([high, low], axis=1), TN)
            state[d] = updated

            @pl.when(it == ITERS - 1)
            def _():
                @pl.when(d > 0)
                def _():
                    ret_tx[d] = updated.astype(BF)

                @pl.when(d == 0)
                def _():
                    ret_rx[0] = updated.astype(BF)

        loop(0, n, update)
        inj_all[me] = (inj_acc[:, :hours] + inj_acc[:, hours:] - demand[...]).astype(BF)

        loop(0, depth - 1, lambda k: c4(k).start())
        c5(depth - 1).start()
        c6(depth - 1).start()

        @pl.when(it == ITERS - 1)
        def _():
            loop(1, n, lambda d: ret_copy(d).start())

        flow[...] = jnp.zeros_like(flow)
        bal[...] = jnp.zeros_like(bal)
        tile = lines // 5

        def use(o):
            block = inj_all[o]
            bal[...] += jnp.sum(
                block.astype(F32).reshape(buses // 8, 8, hours), axis=0
            )

            def rows(i):
                here = pl.ds(pl.multiple_of(i * tile, tile), tile)
                flow[here, :] += dot(pt[o, here, :], block)

            loop(0, 5, rows)

        def y_part(k):
            c5(k).wait_recv()
            c6y(k).start()
            use(at(z_from(k), 1 - y, c))
            c6y(k).wait_recv()
            use(at(z_from(k), 1 - y, 1 - c))

        use(me)
        c6(depth - 1).wait_recv()
        use(at(z, y, 1 - c))

        def arrive(k):
            @pl.when(k < depth - 1)
            def _():
                c4(k).wait_recv()
                c5(k).start()
                c6(k).start()
                use(at(z_from(k), y, c))

            y_part(lax.rem(k + depth - 1, depth))

            @pl.when(k < depth - 1)
            def _():
                c6(k).wait_recv()
                use(at(z_from(k), y, 1 - c))

        loop(0, depth, arrive)

        shifted = line_out[...] + sigma_step * flow[...]
        bound = limit[...]
        line_out[...] = shifted - sigma_step * jnp.clip(
            shifted / sigma_step, -bound, bound
        )
        balance_out[...] = balance_out[...] + sigma_step * jnp.sum(
            bal[...], axis=0, keepdims=True
        ) / (n * buses)

        loop(0, depth - 1, lambda k: c4(k).wait_send())

        def sent_ag(k):
            c5(k).wait_send()
            c6(k).wait_send()
            c6y(k).wait_send()

        loop(0, depth, sent_ag)

    loop(0, ITERS, iterate)

    dispatch_out[...] = jnp.zeros_like(dispatch_out)

    def collect(d):
        @pl.when(d > 0)
        def _():
            ret_copy(d).wait_recv()

        dispatch_out[...] += dot(pick[d], ret_rx[d], TN)

    loop(0, n, collect)

    def sent(d):
        gen_copy(d).wait_send()
        ret_copy(d).wait_send()

    loop(1, n, sent)


def local(
    ptdf,
    line_limit,
    gen_cost,
    gen_max,
    gen_owner,
    gen_local,
    availability,
    demand,
    dispatch,
    balance_price,
    line_price,
):
    n = lax.axis_size("bus")
    buses = demand.shape[0]
    lines, hours = line_price.shape
    gens = dispatch.shape[0]
    capacity = -(-max(2, 3 * gens // n) // 16) * 16
    wide = max(2 * hours, -(-capacity // 128) * 128)
    depth = n // 4
    flat = buses % 128 == 0
    if not flat:
        ptdf = ptdf.reshape(lines, n, buses).transpose(1, 0, 2)
    gen_rows = jnp.concatenate(
        [
            gen_owner.reshape(1, gens).astype(F32),
            gen_local.reshape(1, gens).astype(F32),
            gen_cost.reshape(1, gens),
            jnp.zeros((5, gens), F32),
        ],
        axis=0,
    )
    vmem = pl.BlockSpec(memory_space=pltpu.VMEM)
    dma = pltpu.SemaphoreType.DMA
    block = (hours, buses)
    out = pl.pallas_call(
        functools.partial(kernel, n, capacity, flat),
        out_shape=(
            jax.ShapeDtypeStruct((gens, hours), F32),
            jax.ShapeDtypeStruct((1, hours), F32),
            jax.ShapeDtypeStruct((lines, hours), F32),
        ),
        in_specs=[pl.BlockSpec(memory_space=pl.ANY)] + [vmem] * 8,
        out_specs=(vmem, vmem, vmem),
        scratch_shapes=[
            pltpu.VMEM((n, lines, buses), BF),
            pltpu.VMEM((hours, lines), BF),
            pltpu.VMEM((2 * depth,) + block, BF),
            pltpu.VMEM((2 * depth,) + block, F32),
            pltpu.VMEM((2 * depth,) + block, BF),
            pltpu.VMEM((depth,) + block, BF),
            pltpu.VMEM((depth,) + block, BF),
            pltpu.VMEM((depth,) + block, BF),
            pltpu.VMEM((depth,) + block, BF),
            pltpu.VMEM(block, F32),
            pltpu.VMEM((n, buses, hours), BF),
            pltpu.VMEM((buses, 2 * hours), F32),
            pltpu.VMEM((lines, hours), F32),
            pltpu.VMEM((8, hours), F32),
            pltpu.VMEM((n, capacity, gens), BF),
            pltpu.VMEM((n, capacity + 16, wide), BF),
            pltpu.VMEM((n, capacity + 16, wide), BF),
            pltpu.VMEM((n, capacity, buses), BF),
            pltpu.VMEM((n, capacity, hours), F32),
            pltpu.VMEM((n, capacity, hours), F32),
            pltpu.VMEM((n, capacity, hours), F32),
            pltpu.VMEM((n, capacity, hours), BF),
            pltpu.VMEM((n, capacity, hours), BF),
            dma((n,)),
            dma((2 * depth,)),
            dma((2 * depth,)),
        ]
        + [dma((depth,))] * 8
        + [dma((2 * depth,))] * 2
        + [dma((n,))] * 4,
        compiler_params=pltpu.CompilerParams(
            collective_id=0, has_side_effects=True, vmem_limit_bytes=63 * 1024 * 1024
        ),
    )(
        ptdf,
        line_limit[:, None],
        gen_rows,
        gen_max[:, None],
        availability,
        demand,
        dispatch,
        balance_price[None, :],
        line_price,
    )
    return out[0], out[1][0], out[2]


def solution(mesh):
    return jax.shard_map(
        local,
        mesh=mesh,
        in_specs=(
            P("bus", None),
            P("bus"),
            P("bus"),
            P("bus"),
            P("bus", None),
            P("bus"),
            P(("cases", "bus"), None),
            P(("cases", "bus"), None),
            P(("cases", "bus"), None),
            P("cases"),
            P(("cases", "bus"), None),
        ),
        out_specs=(P(("cases", "bus"), None), P("cases"), P(("cases", "bus"), None)),
        check_vma=False,
    )
```

time: 594 us -> 183 us (0.31)
  waiting for transfers between devices: 375 us -> 0 us
  Pallas kernels: 0 us -> 171 us
  blocking collectives: 84.8 us -> 0 us
  matrix products: 55.7 us -> 0 us
  other arithmetic: 31.6 us -> 2.05 us
  between operations: 14.5 us -> 0.65 us
  starting transfers between devices: 13.5 us -> 0 us
  local copies, waits for them, and re-layouts: 15.7 us -> 9.05 us
    reduce_scatter x4 -> x0, waiting for transfers between devices: 285 us -> none  [the longest x2 153 us: local(): lax.psum_scatter(full_sums, 'bus', scatter_dimension=0, tiled=True) - demand]
    pallas_call x0 -> x1, Pallas kernels: none -> 171 us  [local(): pl.pallas_call(functools.partial(kernel, n, capacity, flat), out_shape=(j...]
    psum x2 -> x0, blocking collectives: 68.2 us -> none  [local(): balance = lax.psum(jnp.sum(injection, axis=0), 'bus')]
    all_gather x2 -> x0, waiting for transfers between devices: 64.8 us -> none  [local(): lax.all_gather(injection.astype(jnp.bfloat16), 'bus', axis=0, tiled=True)]
    dot_general x4 -> x0, matrix products: 55.7 us -> none  [the longest x2 28.2 us: local(): lax.dot_general(ptdf, line_half, (((0,), (0,)), ((), ())), preferred_elem...]
    all_to_all x2 -> x0, waiting for transfers between devices: 25.3 us -> none  [local(): lax.all_to_all(outgoing, 'bus', split_axis=0, concat_axis=0, tiled=True)]
    scatter-add x2 -> x0, other arithmetic: 17.5 us -> none  [local(): full_sums = jax.ops.segment_sum(extra, global_bus, num_segments=all_buses)]
    all_gather x1 -> x0, blocking collectives: 16.6 us -> none  [local(): every_bus = lax.all_gather(global_bus, 'bus', axis=0, tiled=True)]
  transfers between devices with their start and end apart: 8 -> 0, of which waited for: 7 -> 0; matrix products, arithmetic and copies ran while one was open for 1% -> 0% of each run, Pallas kernels for 0% -> 0%
where the time goes in v1:
time: 183 us
  Pallas kernels  171 us (93%)
  local copies, waits for them, and re-layouts  9.05 us (5%)
  other arithmetic  2.05 us (1%)
    pallas_call x1, Pallas kernels, local(): pl.pallas_call(functools.partial(kernel, n, capacity, flat), out_shape=(j...  171 us
    unnamed x3, local copies, waits for them, and re-layouts  4.91 us

profile of v1, /device:TPU:17, one launch (start us, length us, event | category | flops | bytes accessed | tf_op | source)
XLA Modules:
  0.0 183.0 jit_solution(543397429455139402)
XLA Ops:
  0.6 0.1 pad.3.clone
  0.7 0.7 reshape.25
  1.4 0.7 convert_bitcast_fusion
  2.1 0.7 convert_element_type.22
  2.8 0.7 maximum_maximum_fusion.gen_rows_in
  3.5 1.6 broadcast_in_dim.17.gen_max
  5.1 1.8 broadcast_in_dim.16.limit
  6.8 171.3 %shard_map.130 = (f32[768,128]{1,0:T(8,128)}, f32[1,128]{1,0:T(1,128)}, f32[1280,128]{1,0:T(8,128)}) custom-call(bf16[1280,10240]{1,0:T(8,128)(2,1)} %ptdf.1, f32[1280,1]{1,0:T(8,128)} %broadcast_in_dim.16.limit, f32[8,768]{1,0:T(8,128)} %maximum_maximum_fusion.gen_rows_in, f32[768,1]{1,0:T(8,128)} %broadcast_in_dim.17.gen_max, f32[768,128]{1,0:T(8,128)} %availability.1, ...), custom_call_target="tpu_custom_call" | custom-call | tf_op jit(solution)/shard_map/pallas_call | solution.py:502
  178.1 1.8 copy.19
  179.9 1.2 copy.20
  181.1 2.0 %copy.21 = f32[1280,128]{1,0:T(8,128)} copy(f32[1280,128]{1,0:T(8,128)} %get-tuple-element.14) | data formatting | bytes 1310720
  (2 shorter events, 0.0 us)

commit v2 on v1

--- a/solution.py
+++ b/solution.py
@@ -39,7 +39,6 @@
     ptdf,
     limit,
     gen_rows_in,
-    gen_max,
     availability,
     demand,
     dispatch,
@@ -59,7 +58,8 @@
     z_rx,
     shadow_t,
     inj_all,
-    inj_acc,
+    ext,
+    line_now,
     flow,
     bal,
     pick,
@@ -92,6 +92,7 @@
     lines = pt.shape[1]
     buses = pt.shape[2]
     hours = line_in.shape[1]
+    chunk = n // 4 * (gen_tx.shape[1] - 16)
     gens = dispatch.shape[0]
     wide = gen_tx.shape[2]
     depth = n // 4
@@ -159,12 +160,13 @@
     loop(1, n, greet)
     pl.semaphore_wait(barrier, n - 1)
 
-    line_out[...] = line_in[...]
+    line_now[...] = jnp.transpose(line_in[...])
     balance_out[...] = balance_in[...]
 
     owner_row = gen_rows_in[0:1, :]
     local_row = gen_rows_in[1:2, :]
     cost_row = gen_rows_in[2:3, :]
+    top_row = gen_rows_in[3:4, :]
     owner_ids = lax.broadcasted_iota(jnp.int32, (n, gens), 0).astype(F32)
     hits = (owner_ids == owner_row).astype(F32)
     before = (
@@ -175,51 +177,67 @@
     rank_row = jnp.sum(counts * hits, axis=0, keepdims=True)
     local_high = jnp.floor(local_row * (1.0 / 16.0))
     local_low = local_row - 16.0 * local_high
-    cost_a = cost_row.astype(BF).astype(F32)
-    cost_b = (cost_row - cost_a).astype(BF).astype(F32)
-    cost_c = cost_row - cost_a - cost_b
+
+    def parts(x):
+        a = x.astype(BF).astype(F32)
+        b = (x - a).astype(BF).astype(F32)
+        return [a, b, x - a - b]
+
     facts = jnp.concatenate(
         [
             local_high,
             local_low,
             jnp.ones_like(local_row),
-            cost_a,
-            cost_b,
-            cost_c,
-            jnp.zeros((10, gens), F32),
+            *parts(cost_row),
+            *parts(top_row),
+            jnp.zeros((7, gens), F32),
         ],
         axis=0,
     ).astype(BF)
     goods = jnp.concatenate(
-        [dispatch[...].astype(BF), (gen_max[...] * availability[...]).astype(BF)], axis=1
+        [dispatch[...].astype(BF), availability[...].astype(BF)], axis=1
     )
     slot_ids = lax.broadcasted_iota(jnp.int32, (wide, gens), 0).astype(F32)
+
+    def rows_of(d):
+        return pl.ds(pl.multiple_of(d * capacity, 16), capacity)
+
+    def chunk_of(q):
+        return pl.ds(pl.multiple_of(q * chunk, 16), chunk)
 
     def gen_copy(d):
         return remote(
             gen_tx.at[d], gen_rx.at[d], sa.at[d], ra.at[d], lax.rem(me + d, n)
         )
 
-    def send_gens(d):
-        o = lax.rem(me + d, n).astype(F32)
-        where = jnp.where(owner_row == o, rank_row, -1.0)
-        chosen = (slot_ids == where).astype(F32).astype(BF)
-        pick[d] = chosen[:capacity]
-        body = dot(chosen[:capacity], goods).astype(BF)
-        tail = dot(facts, chosen, NT).astype(BF)
-
-        @pl.when(d > 0)
-        def _():
-            gen_tx[d, :capacity] = body
-            gen_tx[d, capacity:] = tail
-            gen_copy(d).start()
-
-        @pl.when(d == 0)
-        def _():
-            gen_rx[0, :capacity] = body
-            gen_rx[0, capacity:] = tail
-
-    loop(0, n, send_gens)
+    def send_gens(q):
+        def choose(i):
+            d = q * depth + i
+            o = lax.rem(me + d, n).astype(F32)
+            where = jnp.where(owner_row == o, rank_row, -1.0)
+            chosen = (slot_ids == where).astype(F32).astype(BF)
+            pick[rows_of(d), :] = chosen[:capacity]
+            gen_tx[d, capacity:] = dot(facts, chosen, NT).astype(BF)
+
+        loop(0, depth, choose)
+        body = dot(pick[chunk_of(q), :], goods).astype(BF)
+        for i in range(depth):
+            gen_tx[q * depth + i, :capacity] = body[i * capacity : (i + 1) * capacity]
+
+        def start(i):
+            d = q * depth + i
+
+            @pl.when(d > 0)
+            def _():
+                gen_copy(d).start()
+
+            @pl.when(d == 0)
+            def _():
+                gen_rx[0] = gen_tx[0]
+
+        loop(0, depth, start)
+
+    loop(0, 4, send_gens)
 
     def take_gens(d):
         @pl.when(d > 0)
@@ -235,12 +253,14 @@
             columns[:, 2:3] > 0.5, columns[:, 0:1] * 16.0 + columns[:, 1:2], -1.0
         )
         ids = lax.broadcasted_iota(jnp.int32, (capacity, buses), 1).astype(F32)
-        seat[d] = (ids == bus).astype(F32).astype(BF)
-        cost[d] = jnp.broadcast_to(
+        here = rows_of(d)
+        seat[here, :] = (ids == bus).astype(F32).astype(BF)
+        cost[here, :] = jnp.broadcast_to(
             columns[:, 3:4] + columns[:, 4:5] + columns[:, 5:6], (capacity, hours)
         )
-        state[d] = gen_rx[d, :capacity, :hours].astype(F32)
-        upper[d] = gen_rx[d, :capacity, hours:].astype(F32)
+        top = columns[:, 6:7] + columns[:, 7:8] + columns[:, 8:9]
+        state[here, :] = gen_rx[d, :capacity, :hours].astype(F32)
+        upper[here, :] = top * gen_rx[d, :capacity, hours:].astype(F32)
 
     def c1(j):
         return remote(part_tx.at[j], core_rx.at[j], s1.at[j], r1.at[j], core_peer)
@@ -269,11 +289,15 @@
 
     def ret_copy(d):
         return remote(
-            ret_tx.at[d], ret_rx.at[d], sb.at[d], rb.at[d], lax.rem(me + n - d, n)
+            ret_tx.at[rows_of(d), :],
+            ret_rx.at[rows_of(d), :],
+            sb.at[d],
+            rb.at[d],
+            lax.rem(me + n - d, n),
         )
 
     def iterate(it):
-        line_t[...] = jnp.transpose(line_out[...]).astype(BF)
+        line_t[...] = line_now[...].astype(BF)
 
         def partial(o):
             @pl.when(it == 0)
@@ -350,29 +374,28 @@
 
         high, low = split(shadow_t[...])
         both = jnp.concatenate([high, low], axis=0)
-        inj_acc[...] = jnp.zeros_like(inj_acc)
-
-        def update(d):
-            found = dot(seat[d], both, NT)
+
+        def update(q):
+            here = chunk_of(q)
+            found = dot(seat[here, :], both, NT)
             price = found[:, :hours] + found[:, hours:] + balance_out[...]
-            now = state[d]
-            updated = jnp.clip(now - tau_step * (cost[d] + price), 0.0, upper[d])
+            now = state[here, :]
+            updated = jnp.clip(
+                now - tau_step * (cost[here, :] + price), 0.0, upper[here, :]
+            )
             high, low = split(2.0 * updated - now)
-            inj_acc[...] += dot(seat[d], jnp.concatenate([high, low], axis=1), TN)
-            state[d] = updated
+            ext[here, :] = jnp.concatenate([high, low], axis=1)
+            state[here, :] = updated
 
             @pl.when(it == ITERS - 1)
             def _():
-                @pl.when(d > 0)
-                def _():
-                    ret_tx[d] = updated.astype(BF)
-
-                @pl.when(d == 0)
-                def _():
-                    ret_rx[0] = updated.astype(BF)
-
-        loop(0, n, update)
-        inj_all[me] = (inj_acc[:, :hours] + inj_acc[:, hours:] - demand[...]).astype(BF)
+                ret_tx[here, :] = updated.astype(BF)
+
+        loop(0, 4, update)
+        made = dot(ext[...], seat[...], TN)
+        inj_all[me] = (made[:hours] + made[hours:] - jnp.transpose(demand[...])).astype(
+            BF
+        )
 
         loop(0, depth - 1, lambda k: c4(k).start())
         c5(depth - 1).start()
@@ -380,23 +403,16 @@
 
         @pl.when(it == ITERS - 1)
         def _():
+            ret_rx[:capacity, :] = ret_tx[:capacity, :]
             loop(1, n, lambda d: ret_copy(d).start())
 
         flow[...] = jnp.zeros_like(flow)
         bal[...] = jnp.zeros_like(bal)
-        tile = lines // 5
 
         def use(o):
             block = inj_all[o]
-            bal[...] += jnp.sum(
-                block.astype(F32).reshape(buses // 8, 8, hours), axis=0
-            )
-
-            def rows(i):
-                here = pl.ds(pl.multiple_of(i * tile, tile), tile)
-                flow[here, :] += dot(pt[o, here, :], block)
-
-            loop(0, 5, rows)
+            bal[...] += block.astype(F32)
+            flow[...] += dot(block, pt[o], NT)
 
         def y_part(k):
             c5(k).wait_recv()
@@ -426,14 +442,13 @@
 
         loop(0, depth, arrive)
 
-        shifted = line_out[...] + sigma_step * flow[...]
+        shifted = line_now[...] + sigma_step * flow[...]
         bound = limit[...]
-        line_out[...] = shifted - sigma_step * jnp.clip(
+        line_now[...] = shifted - sigma_step * jnp.clip(
             shifted / sigma_step, -bound, bound
         )
-        balance_out[...] = balance_out[...] + sigma_step * jnp.sum(
-            bal[...], axis=0, keepdims=True
-        ) / (n * buses)
+        surplus = jnp.sum(jnp.transpose(bal[...]), axis=0, keepdims=True)
+        balance_out[...] = balance_out[...] + sigma_step * surplus / (n * buses)
 
         loop(0, depth - 1, lambda k: c4(k).wait_send())
 
@@ -446,16 +461,9 @@
 
     loop(0, ITERS, iterate)
 
-    dispatch_out[...] = jnp.zeros_like(dispatch_out)
-
-    def collect(d):
-        @pl.when(d > 0)
-        def _():
-            ret_copy(d).wait_recv()
-
-        dispatch_out[...] += dot(pick[d], ret_rx[d], TN)
-
-    loop(0, n, collect)
+    line_out[...] = jnp.transpose(line_now[...])
+    loop(1, n, lambda d: ret_copy(d).wait_recv())
+    dispatch_out[...] = jnp.transpose(dot(ret_rx[...], pick[...], TN))
 
     def sent(d):
         gen_copy(d).wait_send()
@@ -492,7 +500,8 @@
             gen_owner.reshape(1, gens).astype(F32),
             gen_local.reshape(1, gens).astype(F32),
             gen_cost.reshape(1, gens),
-            jnp.zeros((5, gens), F32),
+            gen_max.reshape(1, gens),
+            jnp.zeros((4, gens), F32),
         ],
         axis=0,
     )
@@ -506,7 +515,7 @@
             jax.ShapeDtypeStruct((1, hours), F32),
             jax.ShapeDtypeStruct((lines, hours), F32),
         ),
-        in_specs=[pl.BlockSpec(memory_space=pl.ANY)] + [vmem] * 8,
+        in_specs=[pl.BlockSpec(memory_space=pl.ANY)] + [vmem] * 7,
         out_specs=(vmem, vmem, vmem),
         scratch_shapes=[
             pltpu.VMEM((n, lines, buses), BF),
@@ -519,19 +528,20 @@
             pltpu.VMEM((depth,) + block, BF),
             pltpu.VMEM((depth,) + block, BF),
             pltpu.VMEM(block, F32),
-            pltpu.VMEM((n, buses, hours), BF),
-            pltpu.VMEM((buses, 2 * hours), F32),
-            pltpu.VMEM((lines, hours), F32),
-            pltpu.VMEM((8, hours), F32),
-            pltpu.VMEM((n, capacity, gens), BF),
+            pltpu.VMEM((n,) + block, BF),
+            pltpu.VMEM((n * capacity, 2 * hours), BF),
+            pltpu.VMEM((hours, lines), F32),
+            pltpu.VMEM((hours, lines), F32),
+            pltpu.VMEM(block, F32),
+            pltpu.VMEM((n * capacity, gens), BF),
             pltpu.VMEM((n, capacity + 16, wide), BF),
             pltpu.VMEM((n, capacity + 16, wide), BF),
-            pltpu.VMEM((n, capacity, buses), BF),
-            pltpu.VMEM((n, capacity, hours), F32),
-            pltpu.VMEM((n, capacity, hours), F32),
-            pltpu.VMEM((n, capacity, hours), F32),
-            pltpu.VMEM((n, capacity, hours), BF),
-            pltpu.VMEM((n, capacity, hours), BF),
+            pltpu.VMEM((n * capacity, buses), BF),
+            pltpu.VMEM((n * capacity, hours), F32),
+            pltpu.VMEM((n * capacity, hours), F32),
+            pltpu.VMEM((n * capacity, hours), F32),
+            pltpu.VMEM((n * capacity, hours), BF),
+            pltpu.VMEM((n * capacity, hours), BF),
             dma((n,)),
             dma((2 * depth,)),
             dma((2 * depth,)),
@@ -544,9 +554,8 @@
         ),
     )(
         ptdf,
-        line_limit[:, None],
+        line_limit[None, :],
         gen_rows,
-        gen_max[:, None],
         availability,
         demand,
         dispatch,

time: 183 us -> 158 us (0.86)
  Pallas kernels: 171 us -> 147 us
    pallas_call x1, Pallas kernels: 171 us -> 147 us  [local(): pl.pallas_call(functools.partial(kernel, n, capacity, flat), out_shape=(j...]
    broadcast_in_dim x3 -> x2, local copies, waits for them, and re-layouts: 3.37 us -> 1.3 us  [the longest x1 1.29 us: local(): line_limit[None, :]]
where the time goes in v2:
time: 158 us
  Pallas kernels  147 us (93%)
  local copies, waits for them, and re-layouts  8.17 us (5%)
    pallas_call x1, Pallas kernels, local(): pl.pallas_call(functools.partial(kernel, n, capacity, flat), out_shape=(j...  147 us
    unnamed x3, local copies, waits for them, and re-layouts  4.85 us

profile of v2, /device:TPU:17, one launch (start us, length us, event | category | flops | bytes accessed | tf_op | source)
XLA Modules:
  0.0 157.7 jit_solution(6449641324171151247)
XLA Ops:
  0.6 0.7 reshape.28
  1.3 0.7 reshape.29
  2.0 0.7 convert_bitcast_fusion
  2.7 0.7 convert_element_type.22
  3.4 1.3 broadcast_in_dim.9.limit
  4.7 0.6 concatenate.3.gen_rows_in
  5.3 147.5 %shard_map.130 = (f32[768,128]{1,0:T(8,128)}, f32[1,128]{1,0:T(1,128)}, f32[1280,128]{1,0:T(8,128)}) custom-call(bf16[1280,10240]{1,0:T(8,128)(2,1)} %ptdf.1, f32[1,1280]{1,0:T(1,128)} %broadcast_in_dim.9.limit, f32[8,768]{1,0:T(8,128)} %concatenate.3.gen_rows_in, f32[768,128]{1,0:T(8,128)} %availability.1, f32[640,128]{1,0:T(8,128)} %demand.1, ...), custom_call_target="tpu_custom_call" | custom-call | tf_op jit(solution)/shard_map/pallas_call | solution.py:511
  152.8 1.8 %copy.17 = f32[768,128]{1,0:T(8,128)} copy(f32[768,128]{1,0:T(8,128)} %get-tuple-element.12) | data formatting | bytes 786432
  154.6 1.1 copy.18
  155.7 2.0 %copy.19 = f32[1280,128]{1,0:T(8,128)} copy(f32[1280,128]{1,0:T(8,128)} %get-tuple-element.14) | data formatting | bytes 1310720
  (2 shorter events, 0.0 us)

commit v3 on v2

--- a/solution.py
+++ b/solution.py
@@ -237,8 +237,6 @@
 
         loop(0, depth, start)
 
-    loop(0, 4, send_gens)
-
     def take_gens(d):
         @pl.when(d > 0)
         def _():
@@ -351,6 +349,11 @@
                 shadow_t[...] = total
 
         loop(0, depth, far)
+
+        @pl.when(it == 0)
+        def _():
+            loop(0, 4, send_gens)
+
         loop(0, depth, near)
         loop(0, depth, near_finish)
 

time: 158 us -> 163 us (1.032)
  Pallas kernels: 147 us -> 152 us
    pallas_call x1, Pallas kernels: 147 us -> 152 us  [local(): pl.pallas_call(functools.partial(kernel, n, capacity, flat), out_shape=(j...]
where the time goes in v3:
time: 163 us; the launch traced here: 162 us
  Pallas kernels  152 us (93%)
  local copies, waits for them, and re-layouts  8.17 us (5%)
    pallas_call x1, Pallas kernels, local(): pl.pallas_call(functools.partial(kernel, n, capacity, flat), out_shape=(j...  152 us
    unnamed x3, local copies, waits for them, and re-layouts  4.85 us

profile of v3, /device:TPU:17, one launch (start us, length us, event | category | flops | bytes accessed | tf_op | source)
XLA Modules:
  0.0 162.2 jit_solution(17839296605620971222)
XLA Ops:
  0.6 0.7 reshape.28
  1.3 0.7 reshape.29
  2.0 0.7 convert_bitcast_fusion
  2.7 0.7 convert_element_type.22
  3.4 1.3 broadcast_in_dim.9.limit
  4.7 0.6 concatenate.3.gen_rows_in
  5.3 152.0 %shard_map.130 = (f32[768,128]{1,0:T(8,128)}, f32[1,128]{1,0:T(1,128)}, f32[1280,128]{1,0:T(8,128)}) custom-call(bf16[1280,10240]{1,0:T(8,128)(2,1)} %ptdf.1, f32[1,1280]{1,0:T(1,128)} %broadcast_in_dim.9.limit, f32[8,768]{1,0:T(8,128)} %concatenate.3.gen_rows_in, f32[768,128]{1,0:T(8,128)} %availability.1, f32[640,128]{1,0:T(8,128)} %demand.1, ...), custom_call_target="tpu_custom_call" | custom-call | tf_op jit(solution)/shard_map/pallas_call | solution.py:514
  157.3 1.8 %copy.17 = f32[768,128]{1,0:T(8,128)} copy(f32[768,128]{1,0:T(8,128)} %get-tuple-element.12) | data formatting | bytes 786432
  159.1 1.1 copy.18
  160.2 2.0 %copy.19 = f32[1280,128]{1,0:T(8,128)} copy(f32[1280,128]{1,0:T(8,128)} %get-tuple-element.14) | data formatting | bytes 1310720
  (2 shorter events, 0.0 us)
